TPU v7x, 32 devices: a whole 2x2x4 slice. The times are simulated.
32 devices in a mesh: tm: 8 (over y, x, core), col: 4 (over z).
Axes of the slice: x: 2, y: 2, z: 4, core: 2. Of those that a mesh axis runs over, the one named last changes fastest.
Arguments:
- blocks: float32 [32, 512, 512], P('tm', None, 'col'), as said below
- upper: float32 [32, 512, 512], P('tm', None, 'col'), as said below
- arrow: float32 [32, 64, 512], P('tm', None, 'col'), as said below
- tip: float32 [64, 64], replicated, as said below
- rhs: float32 [32, 512], P('tm'), may hold values from -1 to 1
- rhs_fixed: float32 [64], replicated, may hold values from -6 to 6
Outputs:
- solution: float32 [32, 512], P('tm', 'col')
- solution_fixed: float32 [64], replicated
- mean_log_det: float32 [], replicated
Inputs may be any that keep to these rules, and one draw needn't show every extreme that they name: blocks[t] is symmetric for every t, and the matrix Q assembled from blocks, upper, arrow and tip is positive definite. `upper`: Q assembled with these couplings is positive definite. `arrow`: Q assembled with these couplings is positive definite. tip is symmetric, and Q assembled with it is positive definite.
All inputs are finite; a program needn't handle non-finite values.
Results may differ from a plain program's by a relative error of at most 0.0003.
Values sent between devices are 32-bit elements; how exact they have to be, the bound alone decides.
A program may use at most 192 MiB of HBM per device.

v0:
```python
import jax
import jax.numpy as jnp
from jax import lax
from jax.sharding import PartitionSpec as P


def shifted(block, axis, distance):
    devices = range(lax.axis_size(axis))
    route = [(i - distance, i) for i in devices if i - distance in devices]
    return lax.ppermute(block, axis, route)


def broadcast(x, axis, root):
    mine = lax.axis_index(axis) == root
    return lax.psum(jnp.where(mine, x, jnp.zeros_like(x)), axis)


def lower_solve(factor, right_side):
    return lax.linalg.triangular_solve(factor, right_side, left_side=True, lower=True)


def upper_solve(factor, right_side):
    return lax.linalg.triangular_solve(
        factor, right_side, left_side=True, lower=True, transpose_a=True
    )


def cross_product(first_operand, second_operand):
    return lax.dot_general(
        first_operand,
        second_operand,
        (((0,), (0,)), ((), ())),
        precision=lax.Precision.HIGHEST,
        preferred_element_type=jnp.float32,
    )


def apply_matrix(matrix, vector):
    return jnp.dot(
        matrix, vector, precision=lax.Precision.HIGHEST, preferred_element_type=jnp.float32
    )


def blocked_cholesky(matrix):
    order = matrix.shape[0]
    if order <= 128:
        return jnp.linalg.cholesky(matrix)
    half = order // 2
    top_factor = blocked_cholesky(matrix[:half, :half])
    panel = lax.linalg.triangular_solve(
        top_factor, matrix[half:, :half], left_side=False, lower=True, transpose_a=True
    )
    trailing = matrix[half:, half:] - lax.dot_general(
        panel,
        panel,
        (((1,), (1,)), ((), ())),
        precision=lax.Precision.HIGHEST,
        preferred_element_type=jnp.float32,
    )
    bottom_factor = blocked_cholesky(trailing)
    upper_rows = jnp.concatenate([top_factor, jnp.zeros((half, order - half), jnp.float32)], axis=1)
    lower_rows = jnp.concatenate([panel, bottom_factor], axis=1)
    return jnp.concatenate([upper_rows, lower_rows], axis=0)


def log_pivots(factor):
    return 2.0 * jnp.sum(jnp.log(jnp.diagonal(factor)))


def arrow_solve(factor, side_part, right_part):
    solved = lower_solve(factor, jnp.concatenate([side_part.T, right_part[:, None]], axis=1))
    return (solved[:, :-1], solved[:, -1])


def back_value(factor, right_solved, terms):
    return upper_solve(factor, (right_solved - terms)[:, None])[:, 0]


def transposed_coupling(local_part):
    flipped = local_part.T
    return flipped


def whole_panels(low_local, high_local):
    low_whole, high_whole = (low_local, high_local)
    return (low_whole, high_whole)


def per_device(blocks, upper, arrow, tip, rhs, rhs_fixed):
    step_count, node_count, slab_width = blocks.shape
    effect_count = tip.shape[0]
    part_count = lax.axis_size("tm")
    level_count = part_count.bit_length() - 1
    part_index = lax.axis_index("tm")
    offset = lax.axis_index("col") * slab_width
    zero_value = jnp.zeros((), jnp.float32)
    arrows = lax.all_gather(arrow, "col", axis=2, tiled=True)
    received = lax.all_to_all(upper[0], "col", split_axis=0, concat_axis=1, tiled=True)
    coupling = received.T * (part_index > 0).astype(jnp.float32)
    diagonal = blocks[0]
    side_part = arrows[0]
    right_part = rhs[0]
    sent_diag = jnp.zeros((node_count, slab_width), jnp.float32)
    sent_side = jnp.zeros((effect_count, node_count), jnp.float32)
    sent_right = jnp.zeros((node_count,), jnp.float32)
    inner_tip = jnp.zeros((effect_count, effect_count), jnp.float32)
    inner_fixed = jnp.zeros((effect_count,), jnp.float32)
    inner_log = zero_value
    stored_rows = []
    for step_index in range(step_count - 1):
        whole_diag = lax.all_gather(diagonal, "col", axis=1, tiled=True)
        factor = blocked_cholesky(whole_diag)
        inner_log = inner_log + log_pivots(factor)
        panels = lower_solve(factor, jnp.concatenate([coupling, upper[step_index + 1]], axis=1))
        fill_local = panels[:, :slab_width]
        next_local = panels[:, slab_width:]
        side_solved, right_solved = arrow_solve(factor, side_part, right_part)
        fill_whole, next_whole = (
            lax.all_gather(fill_local, "col", axis=1, tiled=True),
            lax.all_gather(next_local, "col", axis=1, tiled=True),
        )
        sent_diag = sent_diag + cross_product(fill_whole, fill_local)
        sent_side = sent_side + cross_product(side_solved, fill_whole)
        sent_right = sent_right + cross_product(fill_whole, right_solved)
        inner_tip = inner_tip + cross_product(side_solved, side_solved)
        inner_fixed = inner_fixed + cross_product(side_solved, right_solved)
        diagonal = blocks[step_index + 1] - cross_product(next_whole, next_local)
        coupling = -cross_product(next_whole, fill_local)
        side_part = arrows[step_index + 1] - cross_product(side_solved, next_whole)
        right_part = rhs[step_index + 1] - cross_product(next_whole, right_solved)
        stored_rows.append((factor, fill_whole, next_whole, side_solved, right_solved))
    got_diag, got_side, got_right = shifted((sent_diag, sent_side, sent_right), "tm", -1)
    diagonal = diagonal - got_diag
    side_part = side_part - got_side
    right_part = right_part - got_right
    interior_sums = lax.psum((inner_tip, inner_fixed, inner_log), "tm")
    tree_diag, tree_coupling = (
        lax.all_gather(diagonal, "col", axis=1, tiled=True),
        lax.all_gather(coupling, "col", axis=1, tiled=True),
    )
    carried = (
        jnp.zeros((effect_count, effect_count), jnp.float32),
        jnp.zeros((effect_count,), jnp.float32),
        zero_value,
    )
    for level_index in range(level_count):
        stride = 1 << level_index
        position = (part_index + 1) % (2 * stride)
        staying = position == 0
        from_upper = shifted(transposed_coupling(tree_coupling), "tm", -stride)
        factor = blocked_cholesky(tree_diag)
        column_count = tree_coupling.shape[1]
        panels = lower_solve(factor, jnp.concatenate([tree_coupling, from_upper], axis=1))
        low_local = panels[:, :column_count]
        high_local = panels[:, column_count:]
        side_solved, right_solved = arrow_solve(factor, side_part, right_part)
        low_whole, high_whole = whole_panels(low_local, high_local)
        own_tip = cross_product(side_solved, side_solved)
        own_fixed = cross_product(side_solved, right_solved)
        own_log = log_pivots(factor)
        downward = (
            cross_product(low_whole, low_local),
            cross_product(side_solved, low_whole),
            cross_product(low_whole, right_solved),
        )
        upward = (
            cross_product(high_whole, high_local),
            -cross_product(high_whole, low_local),
            cross_product(side_solved, high_whole),
            cross_product(high_whole, right_solved),
        )
        upward = upward + (carried[0] + own_tip, carried[1] + own_fixed, carried[2] + own_log)
        from_above = shifted((downward[0], downward[1], downward[2]), "tm", -stride)
        from_below = shifted(upward, "tm", stride)
        tree_diag = tree_diag - from_above[0] - from_below[0]
        tree_coupling = from_below[1]
        side_part = side_part - from_above[1] - from_below[2]
        right_part = right_part - from_above[2] - from_below[3]
        carried = (
            jnp.where(staying, carried[0] + from_below[4], carried[0]),
            jnp.where(staying, carried[1] + from_below[5], carried[1]),
            jnp.where(staying, carried[2] + from_below[6], carried[2]),
        )
    factor = blocked_cholesky(tree_diag)
    side_solved, right_solved = arrow_solve(factor, side_part, right_part)
    root_tip = cross_product(side_solved, side_solved)
    root_fixed = cross_product(side_solved, right_solved)
    root_log = log_pivots(factor)
    order_total = step_count * part_count * node_count + effect_count
    reduced_tip = tip - interior_sums[0] - carried[0] - root_tip
    reduced_fixed = rhs_fixed - interior_sums[1] - carried[1] - root_fixed
    fixed_factor = jnp.linalg.cholesky(reduced_tip)
    candidate = upper_solve(fixed_factor, lower_solve(fixed_factor, reduced_fixed[:, None]))[:, 0]
    log_candidate = interior_sums[2] + carried[2] + root_log + log_pivots(fixed_factor)
    solution_fixed, log_total = (
        broadcast(candidate, "tm", part_count - 1),
        broadcast(log_candidate, "tm", part_count - 1),
    )
    mean_log_det = log_total / order_total
    boundary_value = back_value(factor, right_solved, apply_matrix(side_solved, solution_fixed))
    prior_value = shifted(boundary_value, "tm", 1)
    solved_rows = [boundary_value]
    following = boundary_value
    for step_index in reversed(range(step_count - 1)):
        factor, fill_whole, next_whole, side_solved, right_solved = stored_rows[step_index]
        terms = (
            apply_matrix(fill_whole, prior_value)
            + apply_matrix(next_whole, following)
            + apply_matrix(side_solved, solution_fixed)
        )
        following = back_value(factor, right_solved, terms)
        solved_rows.insert(0, following)
    whole_rows = jnp.stack(solved_rows)
    solution = lax.dynamic_slice_in_dim(whole_rows, offset, slab_width, 1)
    return (solution, solution_fixed, mean_log_det)


def solution(mesh):
    placed = (
        P("tm", None, "col"),
        P("tm", None, "col"),
        P("tm", None, "col"),
        P(),
        P("tm", None),
        P(),
    )
    return jax.shard_map(
        per_device,
        mesh=mesh,
        in_specs=placed,
        out_specs=(P("tm", "col"), P(), P()),
        check_vma=False,
    )
```

profile of v0, /device:TPU:0, one launch (start us, length us, event | category | flops | bytes accessed | tf_op | source)
XLA Modules:
  0.0 1912.6 jit_solution(14677259304609999665)
XLA Ops:
  18.2 13.9 all-to-all-done
  89.1 20.1 %custom-call.78 = f32[2,128,128]{1,2,0:T(8,128)S(1)} custom-call(f32[2,128,128]{2,1,0:T(8,128)S(1)} %get-tuple-element.164), custom_call_target="InvertDiagBlocksLowerTriangular" | custom-call | tf_op jit(solution)/shard_map/triangular_solve/custom-call.3 | solution.py:50
  157.7 40.4 %custom-call.114 = f32[4,128,128]{1,2,0:T(8,128)S(1)} custom-call(f32[4,128,128]{2,1,0:T(8,128)} %copy-done.69), custom_call_target="InvertDiagBlocksLowerTriangular" | custom-call | tf_op jit(solution)/shard_map/triangular_solve/custom-call.9 | solution.py:23
  206.1 21.0 %all_gather.37 = f32[4,64,512]{2,1,0:T(8,128)S(1)} all-gather(f32[4,64,128]{2,1,0:T(8,128)S(1)} %copy-done.72), channel_id=1, replica_groups=mesh['tm'=8,'col'=4] {'col'}, dimensions={2}, use_global_device_ids=true | all-gather | bytes 655360 | tf_op jit(solution)/shard_map/all_gather | solution.py:97
  253.0 13.7 all-gather.17.cloned.1.call-done
  312.1 20.1 %custom-call.83 = f32[2,128,128]{1,2,0:T(8,128)S(1)} custom-call(f32[2,128,128]{2,1,0:T(8,128)S(1)} %get-tuple-element.167), custom_call_target="InvertDiagBlocksLowerTriangular" | custom-call | tf_op jit(solution)/shard_map/triangular_solve/custom-call.3 | solution.py:50
  385.4 40.3 %custom-call.85 = f32[4,128,128]{1,2,0:T(8,128)S(1)} custom-call(f32[4,128,128]{2,1,0:T(8,128)} %copy-done.70), custom_call_target="InvertDiagBlocksLowerTriangular" | custom-call | tf_op jit(solution)/shard_map/triangular_solve/custom-call.5 | solution.py:19
  444.4 17.9 all-gather.19.cloned.1.call-done
  536.4 20.1 %custom-call.87 = f32[2,128,128]{1,2,0:T(8,128)S(1)} custom-call(f32[2,128,128]{2,1,0:T(8,128)S(1)} %get-tuple-element.169), custom_call_target="InvertDiagBlocksLowerTriangular" | custom-call | tf_op jit(solution)/shard_map/triangular_solve/custom-call.3 | solution.py:50
  612.8 39.5 %custom-call.89 = f32[4,128,128]{1,2,0:T(8,128)S(1)} custom-call(f32[4,128,128]{2,1,0:T(8,128)S(1)} %get-tuple-element.170), custom_call_target="InvertDiagBlocksLowerTriangular" | custom-call | tf_op jit(solution)/shard_map/triangular_solve/custom-call.5 | solution.py:19
  725.6 26.3 %all-reduce.22 = (f32[64,64]{1,0:T(8,128)}, f32[64]{0:T(128)}, f32[]{:T(128)}) all-reduce(f32[64,64]{1,0:T(8,128)S(1)} %convolution_add_fusion.6, f32[64]{0:T(128)S(1)} %fusion.32, f32[]{:T(128)S(6)} %add.248), channel_id=1, replica_groups=mesh['tm'=8,'col'=4] {'tm'}, use_global_device_ids=true, to_apply=%region_2.9 | all-reduce | flops 4161 | bytes 33288 | tf_op jit(solution)/shard_map/psum | solution.py:136
  829.6 21.3 %custom-call.91 = f32[2,128,128]{1,2,0:T(8,128)} custom-call(f32[2,128,128]{2,1,0:T(8,128)} %get-tuple-element.171), custom_call_target="InvertDiagBlocksLowerTriangular" | custom-call | tf_op jit(solution)/shard_map/triangular_solve/custom-call.3 | solution.py:50
  861.9 13.2 cholesky.620
  896.6 13.2 cholesky.631
  937.5 39.9 %custom-call.93 = f32[4,128,128]{1,2,0:T(8,128)} custom-call(f32[4,128,128]{2,1,0:T(8,128)S(1)} %get-tuple-element.172), custom_call_target="InvertDiagBlocksLowerTriangular" | custom-call | tf_op jit(solution)/shard_map/triangular_solve/custom-call.6 | solution.py:19
  1080.5 12.5 cholesky.653
  1103.0 20.7 %custom-call.95 = f32[2,128,128]{1,2,0:T(8,128)} custom-call(f32[2,128,128]{2,1,0:T(8,128)S(1)} %get-tuple-element.173), custom_call_target="InvertDiagBlocksLowerTriangular" | custom-call | tf_op jit(solution)/shard_map/triangular_solve/custom-call.3 | solution.py:50
  1134.8 13.2 cholesky.664
  1169.5 13.2 cholesky.675
  1202.3 14.0 while.56
  1216.3 40.7 %custom-call.97 = f32[4,128,128]{1,2,0:T(8,128)} custom-call(f32[4,128,128]{2,1,0:T(8,128)} %get-tuple-element.174), custom_call_target="InvertDiagBlocksLowerTriangular" | custom-call | tf_op jit(solution)/shard_map/triangular_solve/custom-call.6 | solution.py:19
  1316.5 34.0 %collective-permute-done.20 = f32[512]{0:T(512)S(1)} collective-permute-done((f32[512]{0:T(512)S(1)}, f32[512]{0:T(512)S(1)}, u32[]{:S(2)}, u32[]{:S(2)}) %collective-permute-start.20) | collective-permute-done | bytes 2080 | tf_op jit(solution)/shard_map/ppermute | solution.py:10
  1390.0 12.5 cholesky.697
  1410.6 19.9 %custom-call.99 = f32[2,128,128]{1,2,0:T(8,128)S(1)} custom-call(f32[2,128,128]{2,1,0:T(8,128)S(1)} %get-tuple-element.175), custom_call_target="InvertDiagBlocksLowerTriangular" | custom-call | tf_op jit(solution)/shard_map/triangular_solve/custom-call.3 | solution.py:50
  1440.8 13.2 cholesky.708
  1475.5 13.2 cholesky.719
  1509.7 14.0 while.58
  1523.8 40.7 %custom-call.101 = f32[4,128,128]{1,2,0:T(8,128)} custom-call(f32[4,128,128]{2,1,0:T(8,128)} %get-tuple-element.176), custom_call_target="InvertDiagBlocksLowerTriangular" | custom-call | tf_op jit(solution)/shard_map/triangular_solve/custom-call.6 | solution.py:19
  1686.0 20.5 %custom-call.103 = f32[2,128,128]{1,2,0:T(8,128)} custom-call(f32[2,128,128]{2,1,0:T(8,128)S(1)} %get-tuple-element.177), custom_call_target="InvertDiagBlocksLowerTriangular" | custom-call | tf_op jit(solution)/shard_map/triangular_solve/custom-call.3 | solution.py:50
  1741.8 12.5 cholesky.763
  1770.1 14.5 while.60
  1784.6 40.8 %custom-call.111 = f32[4,128,128]{1,2,0:T(8,128)} custom-call(f32[4,128,128]{2,1,0:T(8,128)} %get-tuple-element.184), custom_call_target="InvertDiagBlocksLowerTriangular" | custom-call | tf_op jit(solution)/shard_map/triangular_solve/custom-call.9 | solution.py:23
  (1006 shorter events, 1295.3 us)
Async XLA Ops:
  7.2 37.2 %all-gather.33.cloned.1.call-start = ((), (), s32[]{:S(2)}) async-start(), calls=%async_computation.11 | async-start | bytes 1310720 | tf_op jit(solution)/shard_map/all_gather | solution.py:111
  11.9 20.3 %all-to-all-start = ((f32[4,128,128]{1,2,0:T(8,128)}), f32[4,128,128]{1,2,0:T(8,128)S(1)}, u32[]{:S(2)}, u32[]{:S(2)}) async-start(f32[4,128,128]{1,2,0:T(8,128)} %copy.121), calls=%async_computation | async-start | bytes 524288 | tf_op jit(solution)/shard_map/all_to_all | solution.py:98
  18.2 218.5 %all-gather.15.cloned.1.call-start = ((), (), s32[]{:S(2)}) async-start(), calls=%async_computation.2 | async-start | bytes 1310720 | tf_op jit(solution)/shard_map/all_gather | solution.py:120
  201.3 65.4 %all-gather.17.cloned.1.call-start = ((), (), s32[]{:S(2)}) async-start(), calls=%async_computation.3 | async-start | bytes 1310720 | tf_op jit(solution)/shard_map/all_gather | solution.py:111
  239.5 194.4 %all-gather.13.cloned.1.call-start = ((), (), s32[]{:S(2)}) async-start(), calls=%async_computation.1 | async-start | bytes 1310720 | tf_op jit(solution)/shard_map/all_gather | solution.py:119
  251.8 210.5 %all-gather.19.cloned.1.call-start = ((), (), s32[]{:S(2)}) async-start(), calls=%async_computation.4 | async-start | bytes 1310720 | tf_op jit(solution)/shard_map/all_gather | solution.py:120
  432.4 59.1 %all-gather.21.cloned.1.call-start = ((), (), s32[]{:S(2)}) async-start(), calls=%async_computation.5 | async-start | bytes 1310720 | tf_op jit(solution)/shard_map/all_gather | solution.py:111
  465.2 197.6 %all-gather.25.cloned.1.call-start = ((), (), s32[]{:S(2)}) async-start(), calls=%async_computation.7 | async-start | bytes 1310720 | tf_op jit(solution)/shard_map/all_gather | solution.py:119
  481.8 207.2 %all-gather.23.cloned.1.call-start = ((), (), s32[]{:S(2)}) async-start(), calls=%async_computation.6 | async-start | bytes 1310720 | tf_op jit(solution)/shard_map/all_gather | solution.py:120
  659.1 60.0 %all-gather.27.cloned.1.call-start = ((), (), s32[]{:S(2)}) async-start(), calls=%async_computation.8 | async-start | bytes 1310720 | tf_op jit(solution)/shard_map/all_gather | solution.py:119
  671.9 93.5 %all-gather.31.cloned.1.call-start = ((), (), s32[]{:S(2)}) async-start(), calls=%async_computation.10 | async-start | bytes 1310720 | tf_op jit(solution)/shard_map/all_gather | solution.py:139
  692.8 87.4 %all-gather.29.cloned.1.call-start = ((), (), s32[]{:S(2)}) async-start(), calls=%async_computation.9 | async-start | bytes 1310720 | tf_op jit(solution)/shard_map/all_gather | solution.py:138
  721.9 30.1 %collective-permute-start = (f32[512,128]{0,1:T(8,128)}, f32[512,128]{0,1:T(8,128)}, u32[]{:S(2)}, u32[]{:S(2)}) collective-permute-start(f32[512,128]{0,1:T(8,128)} %convolution_add_fusion), channel_id=1, source_target_pairs={{4,0},{8,4},{12,8},{16,12},{20,16},{24,20},{28,24},{5,1},{9,5},{13... | collective-permute-start | bytes 786440 | tf_op jit(solution)/shard_map/ppermute | solution.py:10
  768.0 226.2 %collective-permute-start.1 = (f32[512,512]{1,0:T(8,128)}, f32[512,512]{1,0:T(8,128)}, u32[]{:S(2)}, u32[]{:S(2)}) collective-permute-start(f32[512,512]{1,0:T(8,128)} %bitcast.1063), channel_id=1, source_target_pairs={{4,0},{8,4},{12,8},{16,12},{20,16},{24,20},{28,24},{5,1},{9,5},{13... | collective-permute-start | bytes 3145736 | tf_op jit(solution)/shard_map/ppermute | solution.py:10
  988.4 283.6 %collective-permute-start.29 = (f32[64]{0:T(128)}, f32[64]{0:T(128)}, u32[]{:S(2)}, u32[]{:S(2)}) collective-permute-start(f32[64]{0:T(128)} %convolution_bitcast_fusion.17), channel_id=1, source_target_pairs={{0,4},{4,8},{8,12},{12,16},{16,20},{20,24},{24,28},{1,5},{5,9},{9,... | collective-permute-start | bytes 776 | tf_op jit(solution)/shard_map/ppermute | solution.py:10
  1011.0 37.1 %collective-permute-start.2 = (f32[512,512]{0,1:T(8,128)S(1)}, f32[512,512]{0,1:T(8,128)S(1)}, u32[]{:S(2)}, u32[]{:S(2)}) collective-permute-start(f32[512,512]{0,1:T(8,128)S(1)} %fusion.112), channel_id=1, source_target_pairs={{4,0},{8,4},{12,8},{16,12},{20,16},{24,20},{28,24},{5,1},{9,5},{13... | collective-permute-start | bytes 3145736 | tf_op jit(solution)/shard_map/ppermute | solution.py:10
  1012.3 35.8 %collective-permute-start.3 = (f32[512,512]{0,1:T(8,128)S(1)}, f32[512,512]{0,1:T(8,128)S(1)}, u32[]{:S(2)}, u32[]{:S(2)}) collective-permute-start(f32[512,512]{0,1:T(8,128)S(1)} %fusion.105), channel_id=1, source_target_pairs={{0,4},{4,8},{8,12},{12,16},{16,20},{20,24},{24,28},{1,5},{5,9},{9,... | collective-permute-start | bytes 3145736 | tf_op jit(solution)/shard_map/ppermute | solution.py:10
  1037.3 239.4 %collective-permute-start.26 = (f32[64,64]{1,0:T(8,128)}, f32[64,64]{1,0:T(8,128)}, u32[]{:S(2)}, u32[]{:S(2)}) collective-permute-start(f32[64,64]{1,0:T(8,128)} %fusion.312), channel_id=1, source_target_pairs={{0,4},{4,8},{8,12},{12,16},{16,20},{20,24},{24,28},{1,5},{5,9},{9,... | collective-permute-start | bytes 49160 | tf_op jit(solution)/shard_map/ppermute | solution.py:10
  1041.0 145.3 %collective-permute-start.4 = (f32[512,512]{1,0:T(8,128)}, f32[512,512]{1,0:T(8,128)}, u32[]{:S(2)}, u32[]{:S(2)}) collective-permute-start(f32[512,512]{1,0:T(8,128)} %convolution_negate_fusion.1), channel_id=1, source_target_pairs={{0,4},{4,8},{8,12},{12,16},{16,20},{20,24},{24,28},{1,5},{5,9},{9,... | collective-permute-start | bytes 3145736 | tf_op jit(solution)/shard_map/ppermute | solution.py:10
  1188.9 94.7 %collective-permute-start.5 = (f32[512,512]{1,0:T(8,128)}, f32[512,512]{1,0:T(8,128)}, u32[]{:S(2)}, u32[]{:S(2)}) collective-permute-start(f32[512,512]{1,0:T(8,128)} %bitcast.1064), channel_id=1, source_target_pairs={{8,0},{12,4},{16,8},{20,12},{24,16},{28,20},{9,1},{13,5},{17,9},{2... | collective-permute-start | bytes 3145736 | tf_op jit(solution)/shard_map/ppermute | solution.py:10
  1277.6 306.5 %collective-permute-start.27 = (f32[64,64]{1,0:T(8,128)}, f32[64,64]{1,0:T(8,128)}, u32[]{:S(2)}, u32[]{:S(2)}) collective-permute-start(f32[64,64]{1,0:T(8,128)} %convolution_add_fusion.5), channel_id=1, source_target_pairs={{0,8},{4,12},{8,16},{12,20},{16,24},{20,28},{1,9},{5,13},{9,17},{1... | collective-permute-start | bytes 49160 | tf_op jit(solution)/shard_map/ppermute | solution.py:10
  1300.3 61.5 %collective-permute-start.6 = (f32[512,512]{0,1:T(8,128)S(1)}, f32[512,512]{0,1:T(8,128)S(1)}, u32[]{:S(2)}, u32[]{:S(2)}) collective-permute-start(f32[512,512]{0,1:T(8,128)S(1)} %fusion.98), channel_id=1, source_target_pairs={{8,0},{12,4},{16,8},{20,12},{24,16},{28,20},{9,1},{13,5},{17,9},{2... | collective-permute-start | bytes 3145736 | tf_op jit(solution)/shard_map/ppermute | solution.py:10
  1301.6 60.2 %collective-permute-start.7 = (f32[512,512]{0,1:T(8,128)S(1)}, f32[512,512]{0,1:T(8,128)S(1)}, u32[]{:S(2)}, u32[]{:S(2)}) collective-permute-start(f32[512,512]{0,1:T(8,128)S(1)} %fusion.91), channel_id=1, source_target_pairs={{0,8},{4,12},{8,16},{12,20},{16,24},{20,28},{1,9},{5,13},{9,17},{1... | collective-permute-start | bytes 3145736 | tf_op jit(solution)/shard_map/ppermute | solution.py:10
  1306.9 43.7 %collective-permute-start.20 = (f32[512]{0:T(512)S(1)}, f32[512]{0:T(512)S(1)}, u32[]{:S(2)}, u32[]{:S(2)}) collective-permute-start(f32[512]{0:T(512)S(1)} %bitcast.1139), channel_id=1, source_target_pairs={{8,0},{12,4},{16,8},{20,12},{24,16},{28,20},{9,1},{13,5},{17,9},{2... | collective-permute-start | bytes 6152 | tf_op jit(solution)/shard_map/ppermute | solution.py:10
  1308.2 44.7 %collective-permute-start.21 = (f32[512]{0:T(512)S(1)}, f32[512]{0:T(512)S(1)}, u32[]{:S(2)}, u32[]{:S(2)}) collective-permute-start(f32[512]{0:T(512)S(1)} %bitcast.1142), channel_id=1, source_target_pairs={{0,8},{4,12},{8,16},{12,20},{16,24},{20,28},{1,9},{5,13},{9,17},{1... | collective-permute-start | bytes 6152 | tf_op jit(solution)/shard_map/ppermute | solution.py:10
  1355.9 136.4 %collective-permute-start.8 = (f32[512,512]{1,0:T(8,128)}, f32[512,512]{1,0:T(8,128)}, u32[]{:S(2)}, u32[]{:S(2)}) collective-permute-start(f32[512,512]{1,0:T(8,128)} %convolution_negate_fusion), channel_id=1, source_target_pairs={{0,8},{4,12},{8,16},{12,20},{16,24},{20,28},{1,9},{5,13},{9,17},{1... | collective-permute-start | bytes 3145736 | tf_op jit(solution)/shard_map/ppermute | solution.py:10
  1494.9 92.0 %collective-permute-start.9 = (f32[512,512]{1,0:T(8,128)}, f32[512,512]{1,0:T(8,128)}, u32[]{:S(2)}, u32[]{:S(2)}) collective-permute-start(f32[512,512]{1,0:T(8,128)} %bitcast.1065), channel_id=1, source_target_pairs={{16,0},{20,4},{24,8},{28,12},{17,1},{21,5},{25,9},{29,13},{18,2},{... | collective-permute-start | bytes 3145736 | tf_op jit(solution)/shard_map/ppermute | solution.py:10
  1564.5 21.2 %collective-permute-start.35 = (f32[]{:T(128)}, f32[]{:T(128)}, u32[]{:S(2)}, u32[]{:S(2)}) collective-permute-start(f32[]{:T(128)} %add.251), channel_id=1, source_target_pairs={{0,16},{4,20},{8,24},{12,28},{1,17},{5,21},{9,25},{13,29},{2,18},{... | collective-permute-start | bytes 20 | tf_op jit(solution)/shard_map/ppermute | solution.py:10
  1580.0 275.0 %collective-permute-start.31 = (f32[64]{0:T(128)}, f32[64]{0:T(128)}, u32[]{:S(2)}, u32[]{:S(2)}) collective-permute-start(f32[64]{0:T(128)} %fusion.34), channel_id=1, source_target_pairs={{0,16},{4,20},{8,24},{12,28},{1,17},{5,21},{9,25},{13,29},{2,18},{... | collective-permute-start | bytes 776 | tf_op jit(solution)/shard_map/ppermute | solution.py:10
  1602.9 35.2 %collective-permute-start.10 = (f32[512,512]{0,1:T(8,128)S(1)}, f32[512,512]{0,1:T(8,128)S(1)}, u32[]{:S(2)}, u32[]{:S(2)}) collective-permute-start(f32[512,512]{0,1:T(8,128)S(1)} %fusion.84), channel_id=1, source_target_pairs={{16,0},{20,4},{24,8},{28,12},{17,1},{21,5},{25,9},{29,13},{18,2},{... | collective-permute-start | bytes 3145736 | tf_op jit(solution)/shard_map/ppermute | solution.py:10
  1604.4 33.8 %collective-permute-start.11 = (f32[512,512]{0,1:T(8,128)S(1)}, f32[512,512]{0,1:T(8,128)S(1)}, u32[]{:S(2)}, u32[]{:S(2)}) collective-permute-start(f32[512,512]{0,1:T(8,128)S(1)} %fusion.78), channel_id=1, source_target_pairs={{0,16},{4,20},{8,24},{12,28},{1,17},{5,21},{9,25},{13,29},{2,18},{... | collective-permute-start | bytes 3145736 | tf_op jit(solution)/shard_map/ppermute | solution.py:10
  1632.0 201.7 %collective-permute-start.28 = (f32[64,64]{1,0:T(8,128)}, f32[64,64]{1,0:T(8,128)}, u32[]{:S(2)}, u32[]{:S(2)}) collective-permute-start(f32[64,64]{1,0:T(8,128)} %convolution_add_fusion.4), channel_id=1, source_target_pairs={{0,16},{4,20},{8,24},{12,28},{1,17},{5,21},{9,25},{13,29},{2,18},{... | collective-permute-start | bytes 49160 | tf_op jit(solution)/shard_map/ppermute | solution.py:10
  (119 other events, 3464.3 us)
Sparse Core Ops, SparseCore 0:
  10.3 33.9 all-gather.32
  201.4 35.2 all-gather.14
  239.6 27.0 all-gather.16
  268.1 29.7 all-gather.12
  432.6 29.6 all-gather.18
  465.3 26.2 all-gather.20
  493.1 29.6 all-gather.24
  659.3 29.6 all-gather.22
  690.6 28.4 all-gather.26
  720.5 28.4 all-gather.30
  754.8 25.3 all-gather.28
where the time goes:
time: 1940 us; the launch traced here: 1910 us
  other arithmetic  1030 us (53%)
  matrix products  261 us (13%)
  local copies, waits for them, and re-layouts  254 us (13%)
  waiting for transfers between devices  156 us (8%)
  starting transfers between devices  120 us (6%)
  blocking collectives  59.6 us (3%)
  between operations  27.4 us (1%)
    another operation x84, other arithmetic, blocked_cholesky(): return jnp.linalg.cholesky(matrix)  363 us
    another operation x36, other arithmetic, blocked_cholesky(): lax.linalg.triangular_solve(top_factor, matrix[half:, :half], left_side=F...  302 us
    another operation x16, other arithmetic, lower_solve(): lax.linalg.triangular_solve(factor, right_side, left_side=True, lower=True)  204 us
    ppermute x36, starting transfers between devices, shifted(): return lax.ppermute(block, axis, route)  113 us
    another operation x92, matrix products, lower_solve(): lax.linalg.triangular_solve(factor, right_side, left_side=True, lower=True)  92.8 us
    another operation x6, other arithmetic, upper_solve(): lax.linalg.triangular_solve(factor, right_side, left_side=True, lower=Tru...  88.8 us
    dot_general x55, matrix products, cross_product(): lax.dot_general(first_operand, second_operand, (((0,), (0,)), ((), ())),...  78.4 us
    another operation x60, local copies, waits for them, and re-layouts, lower_solve(): lax.linalg.triangular_solve(factor, right_side, left_side=True, lower=True)  62.6 us
  transfers between devices with their start and end apart: 48, of which 16 were waited for; matrix products, arithmetic and copies ran while one was open for 70% of the time, Pallas kernels for 0%

commit v1 on v0

--- a/solution.py
+++ b/solution.py
@@ -1,6 +1,10 @@
+import functools
+
 import jax
 import jax.numpy as jnp
 from jax import lax
+from jax.experimental import pallas as pl
+from jax.experimental.pallas import tpu as pltpu
 from jax.sharding import PartitionSpec as P
 
 
@@ -15,14 +19,18 @@
     return lax.psum(jnp.where(mine, x, jnp.zeros_like(x)), axis)
 
 
-def lower_solve(factor, right_side):
-    return lax.linalg.triangular_solve(factor, right_side, left_side=True, lower=True)
-
-
-def upper_solve(factor, right_side):
-    return lax.linalg.triangular_solve(
-        factor, right_side, left_side=True, lower=True, transpose_a=True
-    )
+def lower_solve(inverse, right_side):
+    return lax.dot_general(
+        inverse,
+        right_side,
+        (((1,), (0,)), ((), ())),
+        precision=lax.Precision.HIGHEST,
+        preferred_element_type=jnp.float32,
+    )
+
+
+def upper_solve(inverse, right_side):
+    return cross_product(inverse, right_side)
 
 
 def cross_product(first_operand, second_operand):
@@ -41,30 +49,105 @@
     )
 
 
-def blocked_cholesky(matrix):
+def eliminate_tile(tile_ref):
+    side = tile_ref.shape[0]
+    rows = lax.broadcasted_iota(jnp.int32, (8, side), 0)
+    cols = lax.broadcasted_iota(jnp.int32, (8, side), 1)
+    for start in range(0, side, 8):
+        strip = tile_ref[start : start + 8, :]
+        entry = {}
+        for j in range(8):
+            spread = jnp.broadcast_to(strip[:, start + j : start + j + 1], (8, side))
+            for i in range(j + 1):
+                entry[i, j] = jnp.broadcast_to(spread[i : i + 1, :], (8, side))
+        inside = (cols >= start) & (cols < start + 8)
+        marked = jnp.where(inside, (cols - start == rows).astype(jnp.float32), strip)
+        solved = jnp.zeros((8, side), jnp.float32)
+        lines = [jnp.broadcast_to(marked[i : i + 1, :], (8, side)) for i in range(8)]
+        for i in range(8):
+            pivot = entry[i, i]
+            scale = lax.rsqrt(pivot)
+            scale = scale * (1.5 - 0.5 * (pivot * scale) * scale)
+            line = lines[i] * scale
+            solved = jnp.where(rows == i, line, solved)
+            factor = {j: entry[i, j] * scale for j in range(i + 1, 8)}
+            for j in range(i + 1, 8):
+                for l in range(j, 8):
+                    entry[j, l] = entry[j, l] - factor[j] * factor[l]
+                lines[j] = lines[j] - factor[j] * line
+        tile_ref[start : start + 8, :] = solved
+        if start + 8 < side:
+            update = lax.dot_general(
+                solved,
+                solved,
+                (((0,), (0,)), ((), ())),
+                precision=lax.Precision.HIGHEST,
+                preferred_element_type=jnp.float32,
+            )
+            below = tile_ref[start + 8 :, :]
+            spot = lax.broadcasted_iota(jnp.int32, below.shape, 1)
+            cleared = (spot >= start) & (spot < start + 8)
+            tile_ref[start + 8 :, :] = jnp.where(cleared, 0.0, below) - update[start + 8 :, :]
+
+
+def inverse_factor_kernel(side, matrix_ref, out_ref, tile_ref):
+    order = matrix_ref.shape[0]
+    count = order // side
+    out_ref[...] = matrix_ref[...]
+
+    @pl.loop(0, count)
+    def _(step):
+        start = pl.multiple_of(step * side, side)
+        here = pl.ds(start, side)
+        tile_ref[...] = out_ref[here, here]
+        eliminate_tile(tile_ref)
+        row = lax.broadcasted_iota(jnp.int32, (side, side), 0)
+        col = lax.broadcasted_iota(jnp.int32, (side, side), 1)
+        inverse = jnp.where(row >= col, tile_ref[...], 0.0)
+        out_ref[here, :] = lax.dot_general(
+            inverse,
+            out_ref[here, :],
+            (((1,), (0,)), ((), ())),
+            precision=lax.Precision.HIGHEST,
+            preferred_element_type=jnp.float32,
+        )
+        out_ref[here, here] = inverse
+
+        @pl.loop(step + 1, count)
+        def _(other):
+            there = pl.ds(pl.multiple_of(other * side, side), side)
+            out_ref[there, here] = jnp.zeros((side, side), jnp.float32)
+            out_ref[there, :] = out_ref[there, :] - lax.dot_general(
+                out_ref[here, there],
+                out_ref[here, :],
+                (((0,), (0,)), ((), ())),
+                precision=lax.Precision.HIGHEST,
+                preferred_element_type=jnp.float32,
+            )
+
+    row = lax.broadcasted_iota(jnp.int32, (order, order), 0)
+    col = lax.broadcasted_iota(jnp.int32, (order, order), 1)
+    out_ref[...] = jnp.where(row >= col, out_ref[...], 0.0)
+
+
+def inverse_factor(matrix):
     order = matrix.shape[0]
-    if order <= 128:
-        return jnp.linalg.cholesky(matrix)
-    half = order // 2
-    top_factor = blocked_cholesky(matrix[:half, :half])
-    panel = lax.linalg.triangular_solve(
-        top_factor, matrix[half:, :half], left_side=False, lower=True, transpose_a=True
-    )
-    trailing = matrix[half:, half:] - lax.dot_general(
-        panel,
-        panel,
-        (((1,), (1,)), ((), ())),
-        precision=lax.Precision.HIGHEST,
-        preferred_element_type=jnp.float32,
-    )
-    bottom_factor = blocked_cholesky(trailing)
-    upper_rows = jnp.concatenate([top_factor, jnp.zeros((half, order - half), jnp.float32)], axis=1)
-    lower_rows = jnp.concatenate([panel, bottom_factor], axis=1)
-    return jnp.concatenate([upper_rows, lower_rows], axis=0)
+    side = min(order, 128)
+    return pl.pallas_call(
+        functools.partial(inverse_factor_kernel, side),
+        out_shape=jax.ShapeDtypeStruct((order, order), jnp.float32),
+        in_specs=[pl.BlockSpec(memory_space=pltpu.VMEM)],
+        out_specs=pl.BlockSpec(memory_space=pltpu.VMEM),
+        scratch_shapes=[pltpu.VMEM((side, side), jnp.float32)],
+        compiler_params=pltpu.CompilerParams(vmem_limit_bytes=32 * 2**20),
+        cost_estimate=pl.CostEstimate(
+            flops=order**3, bytes_accessed=8 * order**2, transcendentals=order
+        ),
+    )(matrix)
 
 
 def log_pivots(factor):
-    return 2.0 * jnp.sum(jnp.log(jnp.diagonal(factor)))
+    return -2.0 * jnp.sum(jnp.log(jnp.diagonal(factor)))
 
 
 def arrow_solve(factor, side_part, right_part):
@@ -109,7 +192,7 @@
     stored_rows = []
     for step_index in range(step_count - 1):
         whole_diag = lax.all_gather(diagonal, "col", axis=1, tiled=True)
-        factor = blocked_cholesky(whole_diag)
+        factor = inverse_factor(whole_diag)
         inner_log = inner_log + log_pivots(factor)
         panels = lower_solve(factor, jnp.concatenate([coupling, upper[step_index + 1]], axis=1))
         fill_local = panels[:, :slab_width]
@@ -148,7 +231,7 @@
         position = (part_index + 1) % (2 * stride)
         staying = position == 0
         from_upper = shifted(transposed_coupling(tree_coupling), "tm", -stride)
-        factor = blocked_cholesky(tree_diag)
+        factor = inverse_factor(tree_diag)
         column_count = tree_coupling.shape[1]
         panels = lower_solve(factor, jnp.concatenate([tree_coupling, from_upper], axis=1))
         low_local = panels[:, :column_count]
@@ -181,7 +264,7 @@
             jnp.where(staying, carried[1] + from_below[5], carried[1]),
             jnp.where(staying, carried[2] + from_below[6], carried[2]),
         )
-    factor = blocked_cholesky(tree_diag)
+    factor = inverse_factor(tree_diag)
     side_solved, right_solved = arrow_solve(factor, side_part, right_part)
     root_tip = cross_product(side_solved, side_solved)
     root_fixed = cross_product(side_solved, right_solved)
@@ -189,7 +272,7 @@
     order_total = step_count * part_count * node_count + effect_count
     reduced_tip = tip - interior_sums[0] - carried[0] - root_tip
     reduced_fixed = rhs_fixed - interior_sums[1] - carried[1] - root_fixed
-    fixed_factor = jnp.linalg.cholesky(reduced_tip)
+    fixed_factor = inverse_factor(reduced_tip)
     candidate = upper_solve(fixed_factor, lower_solve(fixed_factor, reduced_fixed[:, None]))[:, 0]
     log_candidate = interior_sums[2] + carried[2] + root_log + log_pivots(fixed_factor)
     solution_fixed, log_total = (

time: 1940 us -> 943 us (0.49)
  other arithmetic: 1030 us -> 12.7 us
  Pallas kernels: 0 us -> 258 us
  local copies, waits for them, and re-layouts: 254 us -> 77 us
  matrix products: 261 us -> 139 us
  waiting for transfers between devices: 156 us -> 207 us
  starting transfers between devices: 120 us -> 154 us
    another operation x145 -> x0, other arithmetic: 965 us -> none  [the longest x84 363 us: blocked_cholesky(): return jnp.linalg.cholesky(matrix)]
    pallas_call x0 -> x8, Pallas kernels: none -> 258 us  [inverse_factor(): pl.pallas_call(functools.partial(inverse_factor_kernel, side), out_shape=...]
    another operation x156 -> x0, matrix products: 151 us -> none  [the longest x92 92.8 us: lower_solve(): lax.linalg.triangular_solve(factor, right_side, left_side=True, lower=True)]
    another operation x149 -> x0, local copies, waits for them, and re-layouts: 126 us -> none  [the longest x60 62.6 us: lower_solve(): lax.linalg.triangular_solve(factor, right_side, left_side=True, lower=True)]
    all_gather x3, waiting for transfers between devices: 37.1 us -> 74.2 us  [per_device(): lax.all_gather(next_local, 'col', axis=1, tiled=True)]
    ppermute x36, starting transfers between devices: 113 us -> 146 us  [shifted(): return lax.ppermute(block, axis, route)]
    concatenate x16 -> x2, other arithmetic: 24 us -> 0.02 us  [log_pivots(): return -2.0 * jnp.sum(jnp.log(jnp.diagonal(factor)))]
    div x29 -> x0, other arithmetic: 21.1 us -> none  [the longest x28 19.7 us: blocked_cholesky(): return jnp.linalg.cholesky(matrix)]
  transfers between devices with their start and end apart: 48 -> 48, of which waited for: 16 -> 14; matrix products, arithmetic and copies ran while one was open for 70% -> 17% of each run, Pallas kernels for 0% -> 20%
where the time goes in v1:
time: 943 us; the launch traced here: 932 us
  Pallas kernels  258 us (27%)
  waiting for transfers between devices  207 us (22%)
  starting transfers between devices  154 us (16%)
  matrix products  139 us (15%)
  local copies, waits for them, and re-layouts  77 us (8%)
  blocking collectives  58.7 us (6%)
  between operations  25.1 us (3%)
  other arithmetic  12.7 us (1%)
    pallas_call x8, Pallas kernels, inverse_factor(): pl.pallas_call(functools.partial(inverse_factor_kernel, side), out_shape=...  258 us
    ppermute x36, starting transfers between devices, shifted(): return lax.ppermute(block, axis, route)  146 us
    dot_general x60, matrix products, cross_product(): lax.dot_general(first_operand, second_operand, (((0,), (0,)), ((), ())),...  92.6 us
    all_gather x3, waiting for transfers between devices, per_device(): lax.all_gather(next_local, 'col', axis=1, tiled=True)  74.2 us
    ppermute x36, waiting for transfers between devices, shifted(): return lax.ppermute(block, axis, route)  49.7 us
    gather x8, local copies, waits for them, and re-layouts, log_pivots(): return -2.0 * jnp.sum(jnp.log(jnp.diagonal(factor)))  48.8 us
    all_gather x3, waiting for transfers between devices, per_device(): whole_diag = lax.all_gather(diagonal, 'col', axis=1, tiled=True)  40.5 us
    dot_general x14, matrix products, lower_solve(): lax.dot_general(inverse, right_side, (((1,), (0,)), ((), ())), precision=...  36.4 us
  transfers between devices with their start and end apart: 48, of which 14 were waited for; matrix products, arithmetic and copies ran while one was open for 17% of the time, Pallas kernels for 20%

profile of v1, /device:TPU:0, one launch (start us, length us, event | category | flops | bytes accessed | tf_op | source)
XLA Modules:
  0.0 932.1 jit_solution(15377928372889730062)
XLA Ops:
  11.8 6.3 all-to-all-start
  18.1 17.0 %all-to-all-done = f32[4,128,128]{1,2,0:T(8,128)S(1)} async-done(((f32[4,128,128]{1,2,0:T(8,128)}), f32[4,128,128]{1,2,0:T(8,128)S(1)}, u32[]{:S(2)}, u32[]{:S(2)}) %all-to-all-start) | async-done | bytes 262176 | tf_op jit(solution)/shard_map/all_to_all | solution.py:181
  35.1 11.8 %all-gather.33.cloned.1.call-done = f32[1,512,512]{2,1,0:T(8,128)} async-done(((f32[1,512,128]{2,1,0:T(8,128)}), f32[1,512,512]{2,1,0:T(8,128)}) %all-gather.33.cloned.1.call-update) | async-done | bytes 1048592 | tf_op jit(solution)/shard_map/all_gather | solution.py:194
  48.1 36.3 %shard_map.85 = f32[512,512]{1,0:T(8,128)S(1)} custom-call(f32[512,512]{1,0:T(8,128)S(1)} %bitcast.213), custom_call_target="tpu_custom_call" | custom-call | flops 134217728 | bytes 2097152 | tf_op jit(solution)/shard_map/pallas_call | solution.py:136
  87.2 28.1 %all-gather.15.cloned.1.call-done = f32[512,512]{0,1:T(8,128)} async-done(((f32[512,128]{0,1:T(8,128)}), f32[512,512]{0,1:T(8,128)}) %all-gather.15.cloned.1.call-update) | async-done | bytes 1048592 | tf_op jit(solution)/shard_map/all_gather | solution.py:203
  119.6 28.6 %all-gather.17.cloned.1.call-done.matrix_ref = f32[512,512]{1,0:T(8,128)} async-done(((f32[512,128]{1,0:T(8,128)}), f32[512,512]{1,0:T(8,128)}) %all-gather.17.cloned.1.call-update) | async-done | bytes 1048592 | tf_op jit(solution)/shard_map/all_gather | solution.py:194
  149.4 36.3 %shard_map.86 = f32[512,512]{1,0:T(8,128)S(1)} custom-call(f32[512,512]{1,0:T(8,128)S(1)} %copy-done.10), custom_call_target="tpu_custom_call" | custom-call | flops 134217728 | bytes 2097152 | tf_op jit(solution)/shard_map/pallas_call | solution.py:136
  188.6 28.6 %all-gather.19.cloned.1.call-done = f32[512,512]{1,0:T(8,128)} async-done(((f32[512,128]{1,0:T(8,128)}), f32[512,512]{1,0:T(8,128)}) %all-gather.19.cloned.1.call-update) | async-done | bytes 1048592 | tf_op jit(solution)/shard_map/all_gather | solution.py:203
  221.7 19.7 %all_gather.36 = f32[4,64,512]{2,1,0:T(8,128)S(1)} all-gather(f32[4,64,128]{2,1,0:T(8,128)S(1)} %copy-done.44), channel_id=1, replica_groups=mesh['tm'=8,'col'=4] {'col'}, dimensions={2}, use_global_device_ids=true | all-gather | bytes 655360 | tf_op jit(solution)/shard_map/all_gather | solution.py:180
  254.2 36.3 %shard_map.87 = f32[512,512]{1,0:T(8,128)S(1)} custom-call(f32[512,512]{1,0:T(8,128)S(1)} %copy-done.8), custom_call_target="tpu_custom_call" | custom-call | flops 134217728 | bytes 2097152 | tf_op jit(solution)/shard_map/pallas_call | solution.py:136
  326.3 17.5 %all-gather.23.cloned.1.call-done = f32[512,512]{1,0:T(8,128)} async-done(((f32[512,128]{1,0:T(8,128)}), f32[512,512]{1,0:T(8,128)}) %all-gather.23.cloned.1.call-update) | async-done | bytes 1048592 | tf_op jit(solution)/shard_map/all_gather | solution.py:203
  352.1 21.7 %all-gather.27.cloned.1.call-done = f32[512,512]{1,0:T(8,128)} async-done(((f32[512,128]{1,0:T(8,128)}), f32[512,512]{1,0:T(8,128)}) %all-gather.27.cloned.1.call-update) | async-done | bytes 1048592 | tf_op jit(solution)/shard_map/all_gather | solution.py:202
  389.3 26.7 %all-reduce.1 = (f32[64,64]{1,0:T(8,128)}, f32[64]{0:T(128)}, f32[]{:T(128)}) all-reduce(f32[64,64]{1,0:T(8,128)S(1)} %convolution_add_fusion.6, f32[64]{0:T(128)S(1)} %fusion.18, f32[]{:T(128)S(6)} %add.179), channel_id=1, replica_groups=mesh['tm'=8,'col'=4] {'tm'}, use_global_device_ids=true, to_apply=%region_0.1 | all-reduce | flops 4161 | bytes 33288 | tf_op jit(solution)/shard_map/psum | solution.py:219
  435.2 36.3 %shard_map.88 = f32[512,512]{1,0:T(8,128)S(1)} custom-call(f32[512,512]{1,0:T(8,128)S(1)} %copy-done.7), custom_call_target="tpu_custom_call" | custom-call | flops 134217728 | bytes 2097152 | tf_op jit(solution)/shard_map/pallas_call | solution.py:136
  472.5 8.6 gather_fusion.3
  488.5 5.5 fusion
  517.0 17.2 %collective-permute-start.15 = (f32[64,512]{1,0:T(8,128)S(1)}, f32[64,512]{1,0:T(8,128)S(1)}, u32[]{:S(2)}, u32[]{:S(2)}) collective-permute-start(f32[64,512]{1,0:T(8,128)S(1)} %fusion.49), channel_id=1, source_target_pairs={{0,4},{4,8},{8,12},{12,16},{16,20},{20,24},{24,28},{1,5},{5,9},{9,... | collective-permute-start | bytes 393224 | tf_op jit(solution)/shard_map/ppermute | solution.py:14
  540.7 10.6 %collective-permute-start.26 = (f32[64,64]{1,0:T(8,128)S(1)}, f32[64,64]{1,0:T(8,128)S(1)}, u32[]{:S(2)}, u32[]{:S(2)}) collective-permute-start(f32[64,64]{1,0:T(8,128)S(1)} %fusion.113), channel_id=1, source_target_pairs={{0,4},{4,8},{8,12},{12,16},{16,20},{20,24},{24,28},{1,5},{5,9},{9,... | collective-permute-start | bytes 49160 | tf_op jit(solution)/shard_map/ppermute | solution.py:14
  558.1 36.3 %shard_map.89 = f32[512,512]{1,0:T(8,128)S(1)} custom-call(f32[512,512]{1,0:T(8,128)S(1)} %subtract_subtract_fusion.2.matrix_ref), custom_call_target="tpu_custom_call" | custom-call | flops 134217728 | bytes 2097152 | tf_op jit(solution)/shard_map/pallas_call | solution.py:136
  596.5 8.6 gather_fusion.4
  606.4 9.8 %collective-permute-start.34 = (f32[]{:T(128)}, f32[]{:T(128)}, u32[]{:S(2)}, u32[]{:S(2)}) collective-permute-start(f32[]{:T(128)} %add.180), channel_id=1, source_target_pairs={{0,8},{4,12},{8,16},{12,20},{16,24},{20,28},{1,9},{5,13},{9,17},{1... | collective-permute-start | bytes 20 | tf_op jit(solution)/shard_map/ppermute | solution.py:14
  640.8 5.5 collective-permute-start.7
  656.2 32.8 %collective-permute-done.21 = f32[512]{0:T(512)S(1)} collective-permute-done((f32[512]{0:T(512)S(1)}, f32[512]{0:T(512)S(1)}, u32[]{:S(2)}, u32[]{:S(2)}) %collective-permute-start.21) | collective-permute-done | bytes 2080 | tf_op jit(solution)/shard_map/ppermute | solution.py:14
  689.0 22.8 %collective-permute-start.19 = (f32[64,512]{1,0:T(8,128)S(1)}, f32[64,512]{1,0:T(8,128)S(1)}, u32[]{:S(2)}, u32[]{:S(2)}) collective-permute-start(f32[64,512]{1,0:T(8,128)S(1)} %fusion.35), channel_id=1, source_target_pairs={{0,8},{4,12},{8,16},{12,20},{16,24},{20,28},{1,9},{5,13},{9,17},{1... | collective-permute-start | bytes 393224 | tf_op jit(solution)/shard_map/ppermute | solution.py:14
  714.2 5.6 collective-permute-start.27
  726.8 36.3 %shard_map.90 = f32[512,512]{1,0:T(8,128)S(1)} custom-call(f32[512,512]{1,0:T(8,128)S(1)} %subtract_subtract_fusion.1.matrix_ref), custom_call_target="tpu_custom_call" | custom-call | flops 134217728 | bytes 2097152 | tf_op jit(solution)/shard_map/pallas_call | solution.py:136
  765.2 8.6 gather_fusion.5
  775.1 6.8 collective-permute-start.35
  810.1 14.2 %collective-permute-done.25 = f32[512]{0:T(512)S(1)} collective-permute-done((f32[512]{0:T(512)S(1)}, f32[512]{0:T(512)S(1)}, u32[]{:S(2)}, u32[]{:S(2)}) %collective-permute-start.25) | collective-permute-done | bytes 2080 | tf_op jit(solution)/shard_map/ppermute | solution.py:14
  836.8 36.3 %shard_map.91 = f32[512,512]{1,0:T(8,128)S(1)} custom-call(f32[512,512]{1,0:T(8,128)S(1)} %subtract_subtract_fusion.matrix_ref), custom_call_target="tpu_custom_call" | custom-call | flops 134217728 | bytes 2097152 | tf_op jit(solution)/shard_map/pallas_call | solution.py:136
  876.4 8.5 gather_fusion.6
  893.9 12.3 %all-reduce = (f32[64]{0:T(128)S(1)}, f32[]{:T(128)}) all-reduce(f32[64]{0:T(128)S(1)} %fusion.16, f32[]{:T(128)S(6)} %select_n.118), channel_id=1, replica_groups=mesh['tm'=8,'col'=4] {'tm'}, use_global_device_ids=true, to_apply=%region_2.3 | all-reduce | flops 65 | bytes 520 | tf_op jit(solution)/shard_map/psum | solution.py:19
  (322 shorter events, 269.6 us)
Async XLA Ops:
  7.2 39.7 %all-gather.33.cloned.1.call-start = ((), (), s32[]{:S(2)}) async-start(), calls=%async_computation.11 | async-start | bytes 1310720 | tf_op jit(solution)/shard_map/all_gather | solution.py:194
  11.8 23.3 %all-to-all-start = ((f32[4,128,128]{1,2,0:T(8,128)}), f32[4,128,128]{1,2,0:T(8,128)S(1)}, u32[]{:S(2)}, u32[]{:S(2)}) async-start(f32[4,128,128]{1,2,0:T(8,128)} %copy.13), calls=%async_computation | async-start | bytes 524288 | tf_op jit(solution)/shard_map/all_to_all | solution.py:181
  18.1 97.2 %all-gather.15.cloned.1.call-start = ((), (), s32[]{:S(2)}) async-start(), calls=%async_computation.2 | async-start | bytes 1310720 | tf_op jit(solution)/shard_map/all_gather | solution.py:203
  87.2 61.0 %all-gather.17.cloned.1.call-start = ((), (), s32[]{:S(2)}) async-start(), calls=%async_computation.3 | async-start | bytes 1310720 | tf_op jit(solution)/shard_map/all_gather | solution.py:194
  118.4 98.8 %all-gather.19.cloned.1.call-start = ((), (), s32[]{:S(2)}) async-start(), calls=%async_computation.4 | async-start | bytes 1310720 | tf_op jit(solution)/shard_map/all_gather | solution.py:203
  188.5 64.4 %all-gather.21.cloned.1.call-start = ((), (), s32[]{:S(2)}) async-start(), calls=%async_computation.5 | async-start | bytes 1310720 | tf_op jit(solution)/shard_map/all_gather | solution.py:194
  221.0 75.5 %all-gather.13.cloned.1.call-start = ((), (), s32[]{:S(2)}) async-start(), calls=%async_computation.1 | async-start | bytes 1310720 | tf_op jit(solution)/shard_map/all_gather | solution.py:202
  221.6 98.3 %all-gather.25.cloned.1.call-start = ((), (), s32[]{:S(2)}) async-start(), calls=%async_computation.7 | async-start | bytes 1310720 | tf_op jit(solution)/shard_map/all_gather | solution.py:202
  242.3 101.5 %all-gather.23.cloned.1.call-start = ((), (), s32[]{:S(2)}) async-start(), calls=%async_computation.6 | async-start | bytes 1310720 | tf_op jit(solution)/shard_map/all_gather | solution.py:203
  294.1 79.8 %all-gather.27.cloned.1.call-start = ((), (), s32[]{:S(2)}) async-start(), calls=%async_computation.8 | async-start | bytes 1310720 | tf_op jit(solution)/shard_map/all_gather | solution.py:202
  313.2 110.7 %all-gather.31.cloned.1.call-start = ((), (), s32[]{:S(2)}) async-start(), calls=%async_computation.10 | async-start | bytes 1310720 | tf_op jit(solution)/shard_map/all_gather | solution.py:222
  347.6 86.4 %all-gather.29.cloned.1.call-start = ((), (), s32[]{:S(2)}) async-start(), calls=%async_computation.9 | async-start | bytes 1310720 | tf_op jit(solution)/shard_map/all_gather | solution.py:221
  426.4 62.0 %collective-permute-start.1 = (f32[512,512]{1,0:T(8,128)}, f32[512,512]{1,0:T(8,128)}, u32[]{:S(2)}, u32[]{:S(2)}) collective-permute-start(f32[512,512]{1,0:T(8,128)} %bitcast.229), channel_id=1, source_target_pairs={{4,0},{8,4},{12,8},{16,12},{20,16},{24,20},{28,24},{5,1},{9,5},{13... | collective-permute-start | bytes 3145736 | tf_op jit(solution)/shard_map/ppermute | solution.py:14
  502.4 53.5 %collective-permute-start.2 = (f32[512,512]{1,0:T(8,128)}, f32[512,512]{1,0:T(8,128)}, u32[]{:S(2)}, u32[]{:S(2)}) collective-permute-start(f32[512,512]{1,0:T(8,128)} %fusion.59), channel_id=1, source_target_pairs={{4,0},{8,4},{12,8},{16,12},{20,16},{24,20},{28,24},{5,1},{9,5},{13... | collective-permute-start | bytes 3145736 | tf_op jit(solution)/shard_map/ppermute | solution.py:14
  503.8 52.1 %collective-permute-start.3 = (f32[512,512]{1,0:T(8,128)}, f32[512,512]{1,0:T(8,128)}, u32[]{:S(2)}, u32[]{:S(2)}) collective-permute-start(f32[512,512]{1,0:T(8,128)} %fusion.52), channel_id=1, source_target_pairs={{0,4},{4,8},{8,12},{12,16},{16,20},{20,24},{24,28},{1,5},{5,9},{9,... | collective-permute-start | bytes 3145736 | tf_op jit(solution)/shard_map/ppermute | solution.py:14
  508.4 43.7 %collective-permute-start.4 = (f32[512,512]{1,0:T(8,128)S(1)}, f32[512,512]{1,0:T(8,128)}, u32[]{:S(2)}, u32[]{:S(2)}) collective-permute-start(f32[512,512]{1,0:T(8,128)S(1)} %convolution_negate_fusion.1), channel_id=1, source_target_pairs={{0,4},{4,8},{8,12},{12,16},{16,20},{20,24},{24,28},{1,5},{5,9},{9,... | collective-permute-start | bytes 3145736 | tf_op jit(solution)/shard_map/ppermute | solution.py:14
  535.6 82.9 %collective-permute-start.29 = (f32[64]{0:T(128)S(1)}, f32[64]{0:T(128)S(1)}, u32[]{:S(2)}, u32[]{:S(2)}) collective-permute-start(f32[64]{0:T(128)S(1)} %convolution_bitcast_fusion.5), channel_id=1, source_target_pairs={{0,4},{4,8},{8,12},{12,16},{16,20},{20,24},{24,28},{1,5},{5,9},{9,... | collective-permute-start | bytes 776 | tf_op jit(solution)/shard_map/ppermute | solution.py:14
  540.7 83.3 %collective-permute-start.26 = (f32[64,64]{1,0:T(8,128)S(1)}, f32[64,64]{1,0:T(8,128)S(1)}, u32[]{:S(2)}, u32[]{:S(2)}) collective-permute-start(f32[64,64]{1,0:T(8,128)S(1)} %fusion.113), channel_id=1, source_target_pairs={{0,4},{4,8},{8,12},{12,16},{16,20},{20,24},{24,28},{1,5},{5,9},{9,... | collective-permute-start | bytes 49160 | tf_op jit(solution)/shard_map/ppermute | solution.py:14
  554.6 70.9 %collective-permute-start.5 = (f32[512,512]{1,0:T(8,128)}, f32[512,512]{1,0:T(8,128)}, u32[]{:S(2)}, u32[]{:S(2)}) collective-permute-start(f32[512,512]{1,0:T(8,128)} %bitcast.227), channel_id=1, source_target_pairs={{8,0},{12,4},{16,8},{20,12},{24,16},{28,20},{9,1},{13,5},{17,9},{2... | collective-permute-start | bytes 3145736 | tf_op jit(solution)/shard_map/ppermute | solution.py:14
  639.4 85.2 %collective-permute-start.6 = (f32[512,512]{1,0:T(8,128)}, f32[512,512]{1,0:T(8,128)}, u32[]{:S(2)}, u32[]{:S(2)}) collective-permute-start(f32[512,512]{1,0:T(8,128)} %fusion.45), channel_id=1, source_target_pairs={{8,0},{12,4},{16,8},{20,12},{24,16},{28,20},{9,1},{13,5},{17,9},{2... | collective-permute-start | bytes 3145736 | tf_op jit(solution)/shard_map/ppermute | solution.py:14
  640.8 83.8 %collective-permute-start.7 = (f32[512,512]{1,0:T(8,128)}, f32[512,512]{1,0:T(8,128)}, u32[]{:S(2)}, u32[]{:S(2)}) collective-permute-start(f32[512,512]{1,0:T(8,128)} %fusion.38), channel_id=1, source_target_pairs={{0,8},{4,12},{8,16},{12,20},{16,24},{20,28},{1,9},{5,13},{9,17},{1... | collective-permute-start | bytes 3145736 | tf_op jit(solution)/shard_map/ppermute | solution.py:14
  646.3 74.5 %collective-permute-start.8 = (f32[512,512]{1,0:T(8,128)S(1)}, f32[512,512]{1,0:T(8,128)}, u32[]{:S(2)}, u32[]{:S(2)}) collective-permute-start(f32[512,512]{1,0:T(8,128)S(1)} %convolution_negate_fusion), channel_id=1, source_target_pairs={{0,8},{4,12},{8,16},{12,20},{16,24},{20,28},{1,9},{5,13},{9,17},{1... | collective-permute-start | bytes 3145736 | tf_op jit(solution)/shard_map/ppermute | solution.py:14
  651.5 37.5 %collective-permute-start.21 = (f32[512]{0:T(512)S(1)}, f32[512]{0:T(512)S(1)}, u32[]{:S(2)}, u32[]{:S(2)}) collective-permute-start(f32[512]{0:T(512)S(1)} %bitcast.269), channel_id=1, source_target_pairs={{0,8},{4,12},{8,16},{12,20},{16,24},{20,28},{1,9},{5,13},{9,17},{1... | collective-permute-start | bytes 6152 | tf_op jit(solution)/shard_map/ppermute | solution.py:14
  653.4 58.4 %collective-permute-start.20 = (f32[512]{0:T(512)S(1)}, f32[512]{0:T(512)S(1)}, u32[]{:S(2)}, u32[]{:S(2)}) collective-permute-start(f32[512]{0:T(512)S(1)} %bitcast.266), channel_id=1, source_target_pairs={{8,0},{12,4},{16,8},{20,12},{24,16},{28,20},{9,1},{13,5},{17,9},{2... | collective-permute-start | bytes 6152 | tf_op jit(solution)/shard_map/ppermute | solution.py:14
  689.0 25.3 %collective-permute-start.19 = (f32[64,512]{1,0:T(8,128)S(1)}, f32[64,512]{1,0:T(8,128)S(1)}, u32[]{:S(2)}, u32[]{:S(2)}) collective-permute-start(f32[64,512]{1,0:T(8,128)S(1)} %fusion.35), channel_id=1, source_target_pairs={{0,8},{4,12},{8,16},{12,20},{16,24},{20,28},{1,9},{5,13},{9,17},{1... | collective-permute-start | bytes 393224 | tf_op jit(solution)/shard_map/ppermute | solution.py:14
  714.2 72.8 %collective-permute-start.27 = (f32[64,64]{1,0:T(8,128)}, f32[64,64]{1,0:T(8,128)S(1)}, u32[]{:S(2)}, u32[]{:S(2)}) collective-permute-start(f32[64,64]{1,0:T(8,128)} %convolution_add_fusion.5), channel_id=1, source_target_pairs={{0,8},{4,12},{8,16},{12,20},{16,24},{20,28},{1,9},{5,13},{9,17},{1... | collective-permute-start | bytes 49160 | tf_op jit(solution)/shard_map/ppermute | solution.py:14
  723.3 65.9 %collective-permute-start.9 = (f32[512,512]{1,0:T(8,128)}, f32[512,512]{1,0:T(8,128)}, u32[]{:S(2)}, u32[]{:S(2)}) collective-permute-start(f32[512,512]{1,0:T(8,128)} %bitcast.228), channel_id=1, source_target_pairs={{16,0},{20,4},{24,8},{28,12},{17,1},{21,5},{25,9},{29,13},{18,2},{... | collective-permute-start | bytes 3145736 | tf_op jit(solution)/shard_map/ppermute | solution.py:14
  785.0 107.8 %collective-permute-start.31 = (f32[64]{0:T(128)}, f32[64]{0:T(128)}, u32[]{:S(2)}, u32[]{:S(2)}) collective-permute-start(f32[64]{0:T(128)} %fusion.20), channel_id=1, source_target_pairs={{0,16},{4,20},{8,24},{12,28},{1,17},{5,21},{9,25},{13,29},{2,18},{... | collective-permute-start | bytes 776 | tf_op jit(solution)/shard_map/ppermute | solution.py:14
  799.3 37.2 %collective-permute-start.10 = (f32[512,512]{1,0:T(8,128)S(1)}, f32[512,512]{1,0:T(8,128)S(1)}, u32[]{:S(2)}, u32[]{:S(2)}) collective-permute-start(f32[512,512]{1,0:T(8,128)S(1)} %fusion.31), channel_id=1, source_target_pairs={{16,0},{20,4},{24,8},{28,12},{17,1},{21,5},{25,9},{29,13},{18,2},{... | collective-permute-start | bytes 3145736 | tf_op jit(solution)/shard_map/ppermute | solution.py:14
  800.7 35.8 %collective-permute-start.11 = (f32[512,512]{1,0:T(8,128)S(1)}, f32[512,512]{1,0:T(8,128)S(1)}, u32[]{:S(2)}, u32[]{:S(2)}) collective-permute-start(f32[512,512]{1,0:T(8,128)S(1)} %fusion.25), channel_id=1, source_target_pairs={{0,16},{4,20},{8,24},{12,28},{1,17},{5,21},{9,25},{13,29},{2,18},{... | collective-permute-start | bytes 3145736 | tf_op jit(solution)/shard_map/ppermute | solution.py:14
  807.3 21.4 %collective-permute-start.24 = (f32[512]{0:T(512)S(1)}, f32[512]{0:T(512)S(1)}, u32[]{:S(2)}, u32[]{:S(2)}) collective-permute-start(f32[512]{0:T(512)S(1)} %bitcast.267), channel_id=1, source_target_pairs={{16,0},{20,4},{24,8},{28,12},{17,1},{21,5},{25,9},{29,13},{18,2},{... | collective-permute-start | bytes 6152 | tf_op jit(solution)/shard_map/ppermute | solution.py:14
  831.2 53.8 %collective-permute-start.28 = (f32[64,64]{1,0:T(8,128)}, f32[64,64]{1,0:T(8,128)}, u32[]{:S(2)}, u32[]{:S(2)}) collective-permute-start(f32[64,64]{1,0:T(8,128)} %convolution_add_fusion.4), channel_id=1, source_target_pairs={{0,16},{4,20},{8,24},{12,28},{1,17},{5,21},{9,25},{13,29},{2,18},{... | collective-permute-start | bytes 49160 | tf_op jit(solution)/shard_map/ppermute | solution.py:14
  (67 other events, 2180.6 us)
Sparse Core Ops, SparseCore 0:
  9.6 37.2 all-gather.32
  87.3 27.9 all-gather.14
  118.5 29.6 all-gather.16
  188.7 28.4 all-gather.18
  221.2 31.7 all-gather.20
  254.4 27.5 all-gather.12
  283.5 30.1 all-gather.24
  315.2 28.4 all-gather.22
  345.3 28.4 all-gather.26
  375.3 28.5 all-gather.30
  405.4 28.5 all-gather.28
